TPU v7x, 32 devices: a whole 2x2x4 slice. The times are simulated.
32 devices in a mesh: parts: 2 (over y), pencil: 4 (over z), slab: 2 (over x), field: 2 (over core).
Axes of the slice: x: 2, y: 2, z: 4, core: 2. Of those that a mesh axis runs over, the one named last changes fastest.
Arguments:
- state: bfloat16 [16, 2, 512, 512], P('parts', 'slab', 'pencil'), parts along dimension 0, may hold values from -6 to 6
- tangents: bfloat16 [16, 8, 2, 512, 512], P(('parts', 'field'), None, 'slab', 'pencil'), parts along dimension 0, may hold values from -6 to 6
- d1: bfloat16 [512, 512], replicated, may hold values from -0.25 to 0.25
- d2: bfloat16 [512, 512], replicated, may hold values from -0.25 to 0.25
- filt: bfloat16 [512, 512], replicated, may hold values from -0.25 to 0.25
- advect: float32 [2, 8], replicated, may hold values from 0.3 to 1
- diffuse: float32 [8], replicated, may hold values from 0.3 to 1
- coef: float32 [8, 8], replicated, may hold values from -3 to 3
- rates: float32 [8, 8], replicated, may hold values from -3.6 to 3.6
Outputs:
- state_out: bfloat16 [16, 2, 512, 512], P('parts', 'slab', 'pencil'), parts along dimension 0
- tangent_out: bfloat16 [16, 8, 2, 512, 512], P(('parts', 'field'), None, 'slab', 'pencil'), parts along dimension 0
There are 2 independent parts, one for each index of `parts`. A program takes and returns all parts, laid end to end along the dimension named above; an argument that names none is the same for every part. Nothing has to cross between parts.
All inputs are finite; a program needn't handle non-finite values.
Results may differ from a plain program's by a relative error of at most 0.0094.
Values may be sent and summed in bfloat16 or wider, within the bound.
A program may use at most 128 MiB of HBM per device.

v0:
```python
import jax
import jax.numpy as jnp
from jax import lax
from jax.sharding import PartitionSpec as P

highest = lax.Precision.HIGHEST
time_step = 0.4


def spread(values, fields):
    return values.reshape(values.shape + (1,) * (fields.ndim - values.ndim))


def reaction(state, tangent, coef, rates, offset):
    state_float = state.astype(jnp.float32)
    argument = jnp.einsum("ps,s...->p...", rates, state_float, precision=highest)
    activity = jnp.tanh(argument)
    slopes = 1.0 - activity * activity
    state_rate = jnp.einsum("ps,p...->s...", coef, activity, precision=highest)
    tangent_float = tangent.astype(jnp.float32)
    mixing = jnp.einsum("pt,qt...->qp...", rates, tangent_float, precision=highest)
    number = tangent.shape[0]
    own_coef = lax.dynamic_slice_in_dim(coef, offset, number, 0)
    own_activity = lax.dynamic_slice_in_dim(activity, offset, number, 0)
    tangent_rate = jnp.einsum("ps,qp...->qs...", coef, slopes[None] * mixing, precision=highest)
    tangent_rate = tangent_rate + spread(own_coef, tangent) * own_activity[:, None]
    return (state_rate, tangent_rate)


def update(fields, rate, speeds, diffusivity, operators):
    derivative_op, diffusion_op, filter_op = operators
    slope_term = jnp.dot(fields, derivative_op, preferred_element_type=jnp.float32)
    curve_term = jnp.dot(fields, diffusion_op, preferred_element_type=jnp.float32)
    middle = fields.astype(jnp.float32) + time_step * (
        spread(diffusivity, fields) * curve_term - spread(speeds, fields) * slope_term + rate
    )
    middle = middle.astype(jnp.bfloat16)
    return jnp.dot(middle, filter_op, preferred_element_type=jnp.float32).astype(jnp.bfloat16)


def local(state, tangents, d1, d2, filt, advect, diffuse, coef, rates):
    field_index = lax.axis_index("field")
    params_here = tangents.shape[0]
    state_count = state.shape[0]
    offset = field_index * params_here
    operators = (d1, d2, filt)
    for direction in range(2):
        speeds = advect[direction]
        state_rate, tangent_rate = reaction(state, tangents, coef, rates, offset)
        tangents = update(tangents, tangent_rate, speeds[None, :], diffuse[None, :], operators)
        outgoing = update(state, state_rate, speeds, diffuse, operators)
        merged = tangents.reshape((params_here * state_count,) + tangents.shape[2:])
        arrived, merged = (
            lax.all_to_all(outgoing, "pencil", split_axis=3, concat_axis=2, tiled=True),
            lax.all_to_all(merged, "pencil", split_axis=3, concat_axis=2, tiled=True),
        )
        arrived = jnp.swapaxes(arrived, 2, 3)
        merged = jnp.swapaxes(merged, 2, 3)
        tangents = merged.reshape((params_here, state_count) + merged.shape[1:])
        state = arrived
    return (state, tangents)


def solution(mesh):
    in_specs = (
        P("parts", "slab", "pencil", None),
        P(("parts", "field"), None, "slab", "pencil", None),
        P(),
        P(),
        P(),
        P(),
        P(),
        P(),
        P(),
    )
    out_specs = (
        P("parts", "slab", "pencil", None),
        P(("parts", "field"), None, "slab", "pencil", None),
    )
    return jax.shard_map(local, mesh=mesh, in_specs=in_specs, out_specs=out_specs, check_vma=False)
```

profile of v0, /device:TPU:0, one launch (start us, length us, event | category | flops | bytes accessed | tf_op | source)
XLA Modules:
  0.0 366.5 jit_solution(3940533547604179620)
XLA Ops:
  0.6 0.0 copy-start
  0.6 0.0 copy-start.6
  0.7 0.8 slice_bitcast_fusion
  1.5 0.2 copy-done
  1.7 3.2 fusion.76
  5.0 2.1 multiply_subtract_fusion
  7.1 1.3 copy-done.3
  8.4 3.3 fusion.83
  11.7 6.4 %fusion.54 = bf16[8,1,128,512]{3,2,0,1:T(8,128)(2,1)} fusion(f32[128,512,8]{1,2,0:T(8,128)} %fusion.83, f32[8,128,512]{2,1,0:T(8,128)} %fusion.76, bf16[8,1,128,512]{3,2,1,0:T(8,128)(2,1)} %param.9, f32[8]{0:T(128)S(1)} %get-tuple-element.7, f32[8]{0:T(128)S(1)} %copy-done.10, bf16[512,512]{1,0:T(8,128)(2,1)S(1)} %copy-done.9, bf16[512,512]{1,0:T(8,128)(2,1)} %param.11), kind=kOutput, calls=%fused_computation.58 | convolution fusion | flops 1078460416 | bytes 7340096 | tf_op jit(solution)/shard_map/dot_general | solution.py:38
  18.1 2.4 copy.82
  20.5 6.8 %all-to-all-start = ((bf16[8,1,128,512]{2,0,1,3:T(8,128)(2,1)}), bf16[8,1,128,512]{2,0,1,3:T(8,128)(2,1)}, u32[]{:S(2)}, u32[]{:S(2)}) async-start(bf16[8,1,128,512]{2,0,1,3:T(8,128)(2,1)} %copy.82), calls=%async_computation | async-start | bytes 2097152 | tf_op jit(solution)/shard_map/all_to_all | solution.py:54
  27.4 0.0 copy-start.2
  27.4 2.0 constant_dynamic-slice_fusion
  29.4 1.3 copy.93
  30.7 5.7 %fusion.66 = f32[4,8,128,512]{3,2,1,0:T(8,128)} fusion(bf16[512,512]{1,0:T(8,128)(2,1)S(1)} %copy-done, bf16[4,8,1,128,512]{4,3,2,1,0:T(8,128)(2,1)S(1)} %copy-done.2), kind=kOutput, calls=%fused_computation.70 | convolution fusion | flops 2147483648 | bytes 13107200 | tf_op jit(solution)/shard_map/dot_general | solution.py:33
  36.4 5.6 %fusion.21 = f32[4,128,512,8]{2,3,1,0:T(8,128)S(1)} fusion(bf16[4,8,128,512]{3,2,1,0:T(8,128)(2,1)S(1)} %bitcast.280, f32[8,8]{1,0:T(8,128)S(1)} %copy-done.8), kind=kOutput, calls=%fused_computation.22 | convolution fusion | flops 201326592 | bytes 12583168 | tf_op jit(solution)/shard_map/pt,qt...->qp.../dot_general | solution.py:21
  42.0 10.2 %fusion.12 = f32[4,128,512,8]{2,3,1,0:T(8,128)} fusion(f32[4,128,512,8]{2,3,1,0:T(8,128)S(1)} %fusion.21, f32[8,128,512]{2,0,1:T(8,128)S(1)} %get-tuple-element.8, f32[8,8]{1,0:T(8,128)S(1)} %copy-done.7), kind=kOutput, calls=%fused_computation.15 | convolution fusion | flops 203423744 | bytes 18874624 | tf_op jit(solution)/shard_map/ps,qp...->qs.../dot_general | solution.py:25
  52.2 20.5 %fusion.39 = bf16[4,8,128,512]{3,2,1,0:T(8,128)(2,1)} fusion(f32[4,128,512,8]{2,3,1,0:T(8,128)} %fusion.12, f32[4,8,128,512]{3,2,1,0:T(8,128)} %fusion.66, bf16[4,8,1,128,512]{4,3,2,1,0:T(8,128)(2,1)} %param.10, f32[4,128,512]{2,1,0:T(8,128)} %copy.93, f32[4,8]{1,0:T(4,128)S(1)} %constant_dynamic-slice_fusion.1, f32[8]{0:T(128)S(1)} %get-tuple-element.7, ...), kind=kOutput, calls=%fused_computation.37 | convolution fusion | flops 4318035968 | bytes 27263168 | tf_op jit(solution)/shard_map/dot_general | solution.py:38
  72.6 7.9 %copy.94 = bf16[32,1,128,512]{2,0,1,3:T(8,128)(2,1)} copy(bf16[32,1,128,512]{3,2,0,1:T(8,128)(2,1)} %bitcast.285) | data formatting | bytes 8388608 | tf_op jit(solution)/shard_map/reshape | solution.py:52
  80.5 0.0 all-to-all-done
  80.5 5.3 %all-to-all-start.2 = ((bf16[32,1,128,512]{2,0,1,3:T(8,128)(2,1)}), bf16[32,1,128,512]{2,0,1,3:T(8,128)(2,1)}, u32[]{:S(2)}, u32[]{:S(2)}) async-start(bf16[32,1,128,512]{2,0,1,3:T(8,128)(2,1)} %copy.94), calls=%async_computation.2 | async-start | bytes 8388608 | tf_op jit(solution)/shard_map/all_to_all | solution.py:55
  85.9 2.0 copy.151
  87.9 0.4 all_to_all.55
  88.3 0.0 copy-start.5
  88.4 2.0 fusion.74
  90.4 2.7 fusion.49
  93.2 1.4 copy-done.4
  94.5 3.3 fusion.47
  97.8 6.4 %fusion.55 = bf16[8,1,128,512]{3,2,0,1:T(8,128)(2,1)} fusion(f32[128,512,8]{1,2,0:T(8,128)} %fusion.47, f32[8,128,512]{2,1,0:T(8,128)} %fusion.74, bf16[8,1,512,128]{2,3,0,1:T(8,128)(2,1)} %copy-done.5, f32[8]{0:T(128)S(1)} %get-tuple-element.6, f32[8]{0:T(128)S(1)} %copy-done.10, bf16[512,512]{1,0:T(8,128)(2,1)S(1)} %copy-done.9, bf16[512,512]{1,0:T(8,128)(2,1)} %param.11), kind=kOutput, calls=%fused_computation.59 | convolution fusion | flops 1078460416 | bytes 7340096 | tf_op jit(solution)/shard_map/dot_general | solution.py:38
  104.2 2.4 copy.87
  106.7 1.8 dynamic-slice_bitcast_fusion
  108.5 1.3 copy.99
  109.8 69.0 %all-to-all-done.2 = bf16[32,1,128,512]{2,0,1,3:T(8,128)(2,1)} async-done(((bf16[32,1,128,512]{2,0,1,3:T(8,128)(2,1)}), bf16[32,1,128,512]{2,0,1,3:T(8,128)(2,1)}, u32[]{:S(2)}, u32[]{:S(2)}) %all-to-all-start.2) | async-done | bytes 4194336 | tf_op jit(solution)/shard_map/all_to_all | solution.py:55
  178.8 4.7 %all-to-all-start.1 = ((bf16[8,1,128,512]{2,0,1,3:T(8,128)(2,1)}), bf16[8,1,128,512]{2,0,1,3:T(8,128)(2,1)}, u32[]{:S(2)}, u32[]{:S(2)}) async-start(bf16[8,1,128,512]{2,0,1,3:T(8,128)(2,1)} %copy.87), calls=%async_computation.1 | async-start | bytes 2097152 | tf_op jit(solution)/shard_map/all_to_all | solution.py:54
  183.5 7.4 %copy.95 = bf16[32,1,4,128,128]{3,2,4,0,1:T(4,128)(2,1)} copy(bf16[32,1,4,128,128]{3,0,4,2,1:T(8,128)(2,1)} %bitcast.47) | data formatting | bytes 8388608 | tf_op jit(solution)/shard_map/all_to_all | solution.py:55
  190.9 7.2 %all_to_all.63 = bf16[32,1,512,128]{2,3,0,1:T(8,128)(2,1)} reshape(bf16[32,1,4,128,128]{3,2,4,0,1:T(4,128)(2,1)} %copy.95) | data formatting | bytes 8388608 | tf_op jit(solution)/shard_map/all_to_all | solution.py:55
  198.1 8.0 %fusion.19 = f32[4,128,512,8]{2,3,1,0:T(8,128)S(1)} fusion(bf16[4,8,128,512]{3,2,1,0:T(8,128)(2,1)} %bitcast.276, f32[8,8]{1,0:T(8,128)S(1)} %copy-done.8), kind=kOutput, calls=%fused_computation.20 | convolution fusion | flops 201326592 | bytes 12583168 | tf_op jit(solution)/shard_map/pt,qt...->qp.../dot_general | solution.py:21
  206.1 5.6 %fusion.64 = f32[4,8,128,512]{3,2,1,0:T(8,128)} fusion(bf16[4,8,128,512]{3,2,1,0:T(8,128)(2,1)S(1)} %bitcast.279, bf16[512,512]{1,0:T(8,128)(2,1)S(1)} %copy-done), kind=kOutput, calls=%fused_computation.68 | convolution fusion | flops 2147483648 | bytes 13107200 | tf_op jit(solution)/shard_map/dot_general | solution.py:33
  211.7 10.1 %fusion.5 = f32[4,128,512,8]{2,3,1,0:T(8,128)} fusion(f32[4,128,512,8]{2,3,1,0:T(8,128)S(1)} %fusion.19, f32[8,128,512]{2,0,1:T(8,128)S(1)} %get-tuple-element.10, f32[8,8]{1,0:T(8,128)S(1)} %copy-done.7), kind=kOutput, calls=%fused_computation.7 | convolution fusion | flops 203423744 | bytes 18874624 | tf_op jit(solution)/shard_map/ps,qp...->qs.../dot_general | solution.py:25
  221.8 20.3 %fusion.42 = bf16[4,8,128,512]{3,2,1,0:T(8,128)(2,1)} fusion(f32[4,128,512]{2,1,0:T(8,128)} %copy.99, f32[4,128,512,8]{2,3,1,0:T(8,128)} %fusion.5, f32[4,8,128,512]{3,2,1,0:T(8,128)} %fusion.64, bf16[4,8,1,128,512]{4,3,1,0,2:T(8,128)(2,1)} %bitcast.278, f32[8]{0:T(128)S(1)} %get-tuple-element.6, f32[4,8]{1,0:T(4,128)S(1)} %constant_dynamic-slice_fusion.1, ...), kind=kOutput, calls=%fused_computation.38 | convolution fusion | flops 4318035968 | bytes 31457472 | tf_op jit(solution)/shard_map/dot_general | solution.py:38
  242.1 7.9 %copy.100 = bf16[32,1,128,512]{2,0,1,3:T(8,128)(2,1)} copy(bf16[32,1,128,512]{3,2,0,1:T(8,128)(2,1)} %bitcast.284) | data formatting | bytes 8388608 | tf_op jit(solution)/shard_map/reshape | solution.py:52
  250.1 5.3 %all-to-all-start.3 = ((bf16[32,1,128,512]{2,0,1,3:T(8,128)(2,1)}), bf16[32,1,128,512]{2,0,1,3:T(8,128)(2,1)}, u32[]{:S(2)}, u32[]{:S(2)}) async-start(bf16[32,1,128,512]{2,0,1,3:T(8,128)(2,1)} %copy.100), calls=%async_computation.3 | async-start | bytes 8388608 | tf_op jit(solution)/shard_map/all_to_all | solution.py:55
  255.4 2.0 copy.88
  257.4 1.2 all_to_all.59
  258.6 89.2 %all-to-all-done.3 = bf16[32,1,128,512]{2,0,1,3:T(8,128)(2,1)} async-done(((bf16[32,1,128,512]{2,0,1,3:T(8,128)(2,1)}), bf16[32,1,128,512]{2,0,1,3:T(8,128)(2,1)}, u32[]{:S(2)}, u32[]{:S(2)}) %all-to-all-start.3) | async-done | bytes 4194336 | tf_op jit(solution)/shard_map/all_to_all | solution.py:55
  347.8 5.8 %copy.101 = bf16[32,1,128,512]{2,3,0,1:T(8,128)(2,1)} copy(bf16[32,1,128,512]{2,0,1,3:T(8,128)(2,1)} %all-to-all-done.3) | data formatting | bytes 8388608 | tf_op jit(solution)/shard_map/all_to_all | solution.py:55
  353.7 6.5 %copy.102 = bf16[32,1,4,128,128]{4,3,2,0,1:T(8,128)(2,1)} copy(bf16[32,1,4,128,128]{3,4,2,0,1:T(8,128)(2,1)} %bitcast.281) | data formatting | bytes 8388608 | tf_op jit(solution)/shard_map/all_to_all | solution.py:55
  360.1 6.2 %copy.103 = bf16[4,8,1,128,512]{4,3,2,1,0:T(8,128)(2,1)} copy(bf16[4,8,1,128,512]{3,4,1,0,2:T(8,128)(2,1)} %bitcast.282) | data formatting | bytes 8388608
  (17 shorter events, 0.0 us)
Async XLA Ops:
  0.6 1.1 copy-start
  0.6 4.3 %copy-start.6 = (bf16[8,1,128,512]{3,2,1,0:T(8,128)(2,1)S(1)}, bf16[8,1,128,512]{3,2,1,0:T(8,128)(2,1)}, u32[]{:S(2)}) copy-start(bf16[8,1,128,512]{3,2,1,0:T(8,128)(2,1)} %param.9) | copy-start | bytes 3145732
  1.7 6.7 %copy-start.7 = (f32[8,8]{1,0:T(8,128)S(1)}, f32[8,8]{1,0:T(8,128)}, u32[]{:S(2)}) copy-start(f32[8,8]{1,0:T(8,128)} %param.16) | copy-start | bytes 772
  5.0 6.7 %copy-start.9 = (bf16[512,512]{1,0:T(8,128)(2,1)S(1)}, bf16[512,512]{1,0:T(8,128)(2,1)}, u32[]{:S(2)}) copy-start(bf16[512,512]{1,0:T(8,128)(2,1)} %param.13) | copy-start | bytes 1572868
  5.0 6.7 %copy-start.10 = (f32[8]{0:T(128)S(1)}, f32[8]{0:T(128)}, u32[]{:S(2)}) copy-start(f32[8]{0:T(128)} %param.15) | copy-start | bytes 100
  7.1 1.3 copy-start.3
  20.5 60.0 %all-to-all-start = ((bf16[8,1,128,512]{2,0,1,3:T(8,128)(2,1)}), bf16[8,1,128,512]{2,0,1,3:T(8,128)(2,1)}, u32[]{:S(2)}, u32[]{:S(2)}) async-start(bf16[8,1,128,512]{2,0,1,3:T(8,128)(2,1)} %copy.82), calls=%async_computation | async-start | bytes 2097152 | tf_op jit(solution)/shard_map/all_to_all | solution.py:54
  27.4 3.3 copy-start.2
  30.7 5.7 %copy-start.8 = (f32[8,8]{1,0:T(8,128)S(1)}, f32[8,8]{1,0:T(8,128)}, u32[]{:S(2)}) copy-start(f32[8,8]{1,0:T(8,128)} %param.17) | copy-start | bytes 772
  80.5 98.3 %all-to-all-start.2 = ((bf16[32,1,128,512]{2,0,1,3:T(8,128)(2,1)}), bf16[32,1,128,512]{2,0,1,3:T(8,128)(2,1)}, u32[]{:S(2)}, u32[]{:S(2)}) async-start(bf16[32,1,128,512]{2,0,1,3:T(8,128)(2,1)} %copy.94), calls=%async_computation.2 | async-start | bytes 8388608 | tf_op jit(solution)/shard_map/all_to_all | solution.py:55
  88.3 2.1 copy-start.5
  93.2 1.4 copy-start.4
  178.8 71.2 %all-to-all-start.1 = ((bf16[8,1,128,512]{2,0,1,3:T(8,128)(2,1)}), bf16[8,1,128,512]{2,0,1,3:T(8,128)(2,1)}, u32[]{:S(2)}, u32[]{:S(2)}) async-start(bf16[8,1,128,512]{2,0,1,3:T(8,128)(2,1)} %copy.87), calls=%async_computation.1 | async-start | bytes 2097152 | tf_op jit(solution)/shard_map/all_to_all | solution.py:54
  198.1 8.0 %copy-start.1 = (bf16[32,1,512,128]{2,3,0,1:T(8,128)(2,1)S(1)}, bf16[32,1,512,128]{2,3,0,1:T(8,128)(2,1)}, u32[]{:S(2)}) copy-start(bf16[32,1,512,128]{2,3,0,1:T(8,128)(2,1)} %all_to_all.63) | copy-start | bytes 12582916
  250.1 97.8 %all-to-all-start.3 = ((bf16[32,1,128,512]{2,0,1,3:T(8,128)(2,1)}), bf16[32,1,128,512]{2,0,1,3:T(8,128)(2,1)}, u32[]{:S(2)}, u32[]{:S(2)}) async-start(bf16[32,1,128,512]{2,0,1,3:T(8,128)(2,1)} %copy.100), calls=%async_computation.3 | async-start | bytes 8388608 | tf_op jit(solution)/shard_map/all_to_all | solution.py:55
where the time goes:
time: 373 us; the launch traced here: 367 us
  waiting for transfers between devices  158 us (42%)
  matrix products  115 us (31%)
  local copies, waits for them, and re-layouts  69.8 us (19%)
  starting transfers between devices  22.1 us (6%)
    all_to_all x2, waiting for transfers between devices, local(): lax.all_to_all(merged, 'pencil', split_axis=3, concat_axis=2, tiled=True)  158 us
    dot_general x4, matrix products, update(): jnp.dot(middle, filter_op, preferred_element_type=jnp.float32)  53.6 us
    all_to_all x4, local copies, waits for them, and re-layouts, local(): lax.all_to_all(merged, 'pencil', split_axis=3, concat_axis=2, tiled=True)  26.9 us
    dot_general x2, matrix products, reaction(): jnp.einsum('ps,qp...->qs...', coef, slopes[None] * mixing, precision=high...  20.3 us
    dot_general x4, matrix products, update(): jnp.dot(fields, diffusion_op, preferred_element_type=jnp.float32)  16.5 us
    reshape x2, local copies, waits for them, and re-layouts, local(): merged = tangents.reshape((params_here * state_count,) + tangents.shape[2:])  15.8 us
    dot_general x2, matrix products, reaction(): jnp.einsum('pt,qt...->qp...', rates, tangent_float, precision=highest)  13.6 us
    all_to_all x2, starting transfers between devices, local(): lax.all_to_all(outgoing, 'pencil', split_axis=3, concat_axis=2, tiled=True)  11.5 us
  transfers between devices with their start and end apart: 4, of which 2 were waited for; matrix products, arithmetic and copies ran while one was open for 37% of the time, Pallas kernels for 0%

commit v1 on v0

v1 whole, which is shorter than its diff:
```python
import functools

import jax
import jax.numpy as jnp
from jax import lax
from jax.experimental import pallas as pl
from jax.experimental.pallas import tpu as pltpu
from jax.sharding import PartitionSpec as P

time_step = 0.4
MESH = pl.DeviceIdType.MESH
highest = lax.Precision.HIGHEST


def product(left, right):
    return jnp.dot(left, right, preferred_element_type=jnp.float32)


def kernel(
    n, cores, step,
    state_ref, tangent_ref, d1_ref, d2_ref, filt_ref, advect_ref, diffuse_ref, coef_ref, rates_ref,
    state_out, tangent_out,
    rates_hi, rates_lo, coef_mix, coef_own, act, slopes, lines, state_lines, state_end,
    send_s, send_t, take_s, take_t,
    send_sem, take_sem, pass_send, pass_take,
):
    params, count, rows, length = tangent_ref.shape
    width = length // n
    own = count // cores
    me = lax.axis_index("pencil")
    core = lax.axis_index("field")
    first = core * own

    barrier = pltpu.get_barrier_semaphore()
    for d in range(1, n):
        pl.semaphore_signal(barrier, inc=1, device_id={"pencil": lax.rem(me + d, n)}, device_id_type=MESH)
    for d in range(1, cores):
        pl.semaphore_signal(barrier, inc=1, device_id={"field": lax.rem(core + d, cores)}, device_id_type=MESH)

    def picks(height, offset):
        field = lax.broadcasted_iota(jnp.int32, (height, count), 1)
        row = lax.broadcasted_iota(jnp.int32, (height, count), 0)
        return jnp.where(row // step + offset == field, 1.0, 0.0).astype(jnp.float32)

    def spread(matrix, left, right):
        wide = jnp.dot(left, matrix, precision=highest, preferred_element_type=jnp.float32)
        wide = lax.dot_general(wide, right, (((1,), (1,)), ((), ())), precision=highest, preferred_element_type=jnp.float32)
        cell = lax.broadcasted_iota(jnp.int32, wide.shape, 0) % step
        other = lax.broadcasted_iota(jnp.int32, wide.shape, 1) % step
        return jnp.where(cell == other, wide, 0.0)

    all_picks = picks(count * step, 0)
    own_picks = picks(own * step, first)
    rates_wide = spread(rates_ref[...], all_picks, all_picks)
    rates_hi[...] = rates_wide.astype(jnp.bfloat16)
    rates_lo[...] = (rates_wide - rates_hi[...].astype(jnp.float32)).astype(jnp.bfloat16)
    scaled = time_step * coef_ref[...].T
    coef_mix[...] = spread(scaled, all_picks, all_picks).astype(jnp.bfloat16)
    coef_own[...] = spread(scaled, own_picks, all_picks).astype(jnp.bfloat16)

    def rows_of(values, chosen):
        return time_step * jnp.sum(chosen * values, axis=1, keepdims=True)

    pl.semaphore_wait(barrier, n - 1 + cores - 1)

    def move(leg, group, send, take, d):
        dest = lax.rem(me + d, n)
        if d == 0:
            return pltpu.make_async_copy(send.at[me], take.at[me], take_sem.at[leg, group, 0])
        return pltpu.make_async_remote_copy(
            src_ref=send.at[dest], dst_ref=take.at[me],
            send_sem=send_sem.at[leg, group, d], recv_sem=take_sem.at[leg, group, d],
            device_id={"pencil": dest}, device_id_type=MESH,
        )

    def state_move(leg, d):
        return move(leg, 0, send_s.at[leg], take_s.at[leg, core], d)

    def tangent_move(leg, q, d):
        return move(leg, q + 1, send_t.at[leg, q], take_t.at[leg, q], d)

    def arrived(copy, d):
        if d == 0:
            copy.wait()
        else:
            copy.wait_recv()

    def hand_on(which, ref, d):
        return pltpu.make_async_remote_copy(
            src_ref=ref, dst_ref=ref, send_sem=pass_send.at[which, d], recv_sem=pass_take.at[which, d],
            device_id={"field": lax.rem(core + d, cores)}, device_id_type=MESH,
        )

    def finish(fields, rate, speed, spreading, target):
        slope = product(fields, d1_ref[...])
        curve = product(fields, d2_ref[...])
        middle = fields.astype(jnp.float32) + spreading * curve - speed * slope + rate
        result = product(middle.astype(jnp.bfloat16), filt_ref[...]).astype(jnp.bfloat16)
        for j in range(n):
            target(j, result[:, j * width : (j + 1) * width])

    def state_pass(leg, source):
        speed = rows_of(advect_ref[leg : leg + 1, :], own_picks)
        spreading = rows_of(diffuse_ref[...], own_picks)

        @pl.loop(0, rows // step)
        def _(c):
            part = pl.ds(pl.multiple_of(c * step, step), step)
            fields = source[:, part, :].reshape(count * step, length)
            argument = product(rates_hi[...], fields) + product(rates_lo[...], fields)
            activity = jnp.tanh(argument)
            act[c] = activity
            slopes[c] = 1.0 - activity * activity
            rate = product(coef_own[...], activity.astype(jnp.bfloat16))

            def target(j, block):
                send_s[leg, j, :, part, :] = block.reshape(own, step, width)

            mine = source[pl.ds(first, own), part, :].reshape(own * step, length)
            finish(mine, rate, speed, spreading, target)

        for d in range(n):
            state_move(leg, d).start()

    def tangent_pass(leg, q, source):
        speed = rows_of(advect_ref[leg : leg + 1, :], all_picks)
        spreading = rows_of(diffuse_ref[...], all_picks)

        @pl.loop(0, rows // step)
        def _(c):
            part = pl.ds(pl.multiple_of(c * step, step), step)
            fields = source[:, part, :].reshape(count * step, length)
            mixing = product(rates_hi[...], fields)
            channel = lax.broadcasted_iota(jnp.int32, mixing.shape, 0) // step
            direct = jnp.where(channel == core * params + q, act[c], 0.0)
            rate = product(coef_mix[...], (slopes[c] * mixing + direct).astype(jnp.bfloat16))

            def target(j, block):
                send_t[leg, q, j, :, part, :] = block.reshape(count, step, width)

            finish(fields, rate, speed, spreading, target)

        for d in range(n):
            tangent_move(leg, q, d).start()

    def turned(blocks):
        return blocks.reshape(n * blocks.shape[1], width).T

    state_pass(0, state_ref)

    @pl.loop(0, params)
    def _(q):
        tangent_pass(0, q, tangent_ref.at[q])

    for d in range(n):
        arrived(state_move(0, d), d)
    for d in range(1, cores):
        hand_on(0, take_s.at[0, core], d).start()
    for d in range(1, cores):
        hand_on(0, take_s.at[0, core], d).wait_recv()

    @pl.loop(0, cores)
    def _(h):
        @pl.loop(0, own)
        def _(s):
            state_lines[h * own + s] = turned(take_s[0, h, :, s])

    state_pass(1, state_lines)

    @pl.loop(0, params)
    def _(q):
        for d in range(n):
            arrived(tangent_move(0, q, d), d)

        @pl.loop(0, count)
        def _(s):
            lines[s] = turned(take_t[0, q, :, s])

        tangent_pass(1, q, lines)

    for d in range(n):
        arrived(state_move(1, d), d)

    @pl.loop(0, own)
    def _(s):
        state_end[first + s] = turned(take_s[1, core, :, s])

    for d in range(1, cores):
        hand_on(1, state_end.at[pl.ds(first, own)], d).start()

    @pl.loop(0, params)
    def _(q):
        for d in range(n):
            arrived(tangent_move(1, q, d), d)

        @pl.loop(0, count)
        def _(s):
            tangent_out[q, s] = turned(take_t[1, q, :, s])

    for d in range(1, cores):
        hand_on(1, state_end.at[pl.ds(first, own)], d).wait_recv()
    state_out[...] = state_end[...]

    for leg in range(2):
        for d in range(1, n):
            state_move(leg, d).wait_send()
        for d in range(1, cores):
            hand_on(0, take_s.at[0, core], d).wait_send() if leg == 0 else hand_on(
                1, state_end.at[pl.ds(first, own)], d
            ).wait_send()

        @pl.loop(0, params)
        def _(q):
            for d in range(1, n):
                tangent_move(leg, q, d).wait_send()


def local(n, cores, state, tangents, d1, d2, filt, advect, diffuse, coef, rates):
    params, count, planes, rows, length = tangents.shape
    step = 32 if rows % 32 == 0 else rows
    width = length // n
    own = count // cores
    bf16, f32 = jnp.bfloat16, jnp.float32
    spot = pl.BlockSpec(memory_space=pltpu.VMEM)
    cells = params * count * rows * length
    call = pl.pallas_call(
        functools.partial(kernel, n, cores, step),
        out_shape=(
            jax.ShapeDtypeStruct((count, rows, length), bf16),
            jax.ShapeDtypeStruct((params, count, rows, length), bf16),
        ),
        in_specs=[spot] * 9,
        out_specs=(spot, spot),
        scratch_shapes=[
            pltpu.VMEM((count * step, count * step), bf16),
            pltpu.VMEM((count * step, count * step), bf16),
            pltpu.VMEM((count * step, count * step), bf16),
            pltpu.VMEM((own * step, count * step), bf16),
            pltpu.VMEM((rows // step, count * step, length), f32),
            pltpu.VMEM((rows // step, count * step, length), f32),
            pltpu.VMEM((count, width, length), bf16),
            pltpu.VMEM((count, width, length), bf16),
            pltpu.VMEM((count, rows, length), bf16),
            pltpu.VMEM((2, n, own, rows, width), bf16),
            pltpu.VMEM((2, params, n, count, rows, width), bf16),
            pltpu.VMEM((2, cores, n, own, rows, width), bf16),
            pltpu.VMEM((2, params, n, count, rows, width), bf16),
            pltpu.SemaphoreType.DMA((2, params + 1, n)),
            pltpu.SemaphoreType.DMA((2, params + 1, n)),
            pltpu.SemaphoreType.DMA((2, cores)),
            pltpu.SemaphoreType.DMA((2, cores)),
        ],
        compiler_params=pltpu.CompilerParams(
            collective_id=0, has_side_effects=True, vmem_limit_bytes=56 * 2**20
        ),
        cost_estimate=pl.CostEstimate(
            flops=cells * length * 12, bytes_accessed=cells * 4, transcendentals=count * rows * length * 2
        ),
    )
    outs = [
        call(state[:, z], tangents[:, :, z], d1, d2, filt, advect, diffuse[None, :], coef, rates)
        for z in range(planes)
    ]
    return jnp.stack([o[0] for o in outs], 1), jnp.stack([o[1] for o in outs], 2)


def solution(mesh):
    lines = P("parts", "slab", "pencil", None)
    tangent_lines = P(("parts", "field"), None, "slab", "pencil", None)
    return jax.shard_map(
        functools.partial(local, mesh.shape["pencil"], mesh.shape["field"]),
        mesh=mesh,
        in_specs=(lines, tangent_lines) + (P(),) * 7,
        out_specs=(lines, tangent_lines),
        check_vma=False,
    )
```

time: 373 us -> 224 us (0.60); the launches traced: 367 us -> 222 us
  Pallas kernels: 0 us -> 214 us
  waiting for transfers between devices: 158 us -> 0 us
  matrix products: 115 us -> 0 us
  local copies, waits for them, and re-layouts: 69.8 us -> 6.9 us
  starting transfers between devices: 22.1 us -> 0 us
    pallas_call x0 -> x1, Pallas kernels: none -> 214 us  [local(): call(state[:, z], tangents[:, :, z], d1, d2, filt, advect, diffuse[None,...]
    all_to_all x4 -> x0, waiting for transfers between devices: 158 us -> none  [the longest x2 158 us: local(): lax.all_to_all(merged, 'pencil', split_axis=3, concat_axis=2, tiled=True)]
    dot_general x16 -> x0, matrix products: 115 us -> none  [the longest x4 53.6 us: update(): jnp.dot(middle, filter_op, preferred_element_type=jnp.float32)]
    all_to_all x8 -> x0, local copies, waits for them, and re-layouts: 32.6 us -> none  [the longest x4 26.9 us: local(): lax.all_to_all(merged, 'pencil', split_axis=3, concat_axis=2, tiled=True)]
    all_to_all x4 -> x0, starting transfers between devices: 22.1 us -> none  [the longest x2 11.5 us: local(): lax.all_to_all(outgoing, 'pencil', split_axis=3, concat_axis=2, tiled=True)]
    reshape x2 -> x0, local copies, waits for them, and re-layouts: 15.8 us -> none  [local(): merged = tangents.reshape((params_here * state_count,) + tangents.shape[2:])]
    another operation x4 -> x0, local copies, waits for them, and re-layouts: 6.44 us -> none
    convert_element_type x2 -> x0, local copies, waits for them, and re-layouts: 4.87 us -> none  [update(): jnp.dot(middle, filter_op, preferred_element_type=jnp.float32)]
  transfers between devices with their start and end apart: 4 -> 0, of which waited for: 2 -> 0; matrix products, arithmetic and copies ran while one was open for 37% -> 0% of each run, Pallas kernels for 0% -> 0%
where the time goes in v1:
time: 224 us; the launch traced here: 222 us
  Pallas kernels  214 us (96%)
  local copies, waits for them, and re-layouts  6.9 us (3%)
    pallas_call x1, Pallas kernels, local(): call(state[:, z], tangents[:, :, z], d1, d2, filt, advect, diffuse[None,...  214 us
    unnamed x2, local copies, waits for them, and re-layouts  6.9 us

profile of v1, /device:TPU:0, one launch (start us, length us, event | category | flops | bytes accessed | tf_op | source)
XLA Modules:
  0.0 221.9 jit_solution(5723366728475025579)
XLA Ops:
  0.6 214.3 %shard_map.104 = (bf16[8,128,512]{2,1,0:T(8,128)(2,1)}, bf16[4,8,128,512]{3,2,1,0:T(8,128)(2,1)}) custom-call(bf16[8,128,512]{2,1,0:T(8,128)(2,1)} %bitcast.12, bf16[4,8,128,512]{3,2,1,0:T(8,128)(2,1)} %bitcast.11, bf16[512,512]{1,0:T(8,128)(2,1)} %d1_ref.1, bf16[512,512]{1,0:T(8,128)(2,1)} %d2_ref.1, bf16[512,512]{1,0:T(8,128)(2,1)} %filt_ref.1, ...), custom_call_target="tpu_custom_call" | custom-call | flops 12884901888 | bytes 8388608 | tf_op jit(solution)/shard_map/pallas_call | solution.py:261
  215.0 2.3 %copy.15 = bf16[8,1,128,512]{3,2,1,0:T(8,128)(2,1)} copy(bf16[8,1,128,512]{3,2,1,0:T(8,128)(2,1)} %bitcast.10) | data formatting | bytes 2097152
  217.2 4.6 %copy.16 = bf16[4,8,1,128,512]{4,3,2,1,0:T(8,128)(2,1)} copy(bf16[4,8,1,128,512]{4,3,2,1,0:T(8,128)(2,1)} %bitcast.9) | data formatting | bytes 8388608

commit v2 on v1

--- a/solution.py
+++ b/solution.py
@@ -18,11 +18,12 @@
 
 def kernel(
     n, cores, step,
-    state_ref, tangent_ref, d1_ref, d2_ref, filt_ref, advect_ref, diffuse_ref, coef_ref, rates_ref,
+    state_in, tangent_in, d1_in, d2_in, filt_in, advect_ref, diffuse_ref, coef_ref, rates_ref,
     state_out, tangent_out,
+    state_ref, tangent_ref, d1_ref, d2_ref, filt_ref, tangent_end,
     rates_hi, rates_lo, coef_mix, coef_own, act, slopes, lines, state_lines, state_end,
     send_s, send_t, take_s, take_t,
-    send_sem, take_sem, pass_send, pass_take,
+    send_sem, take_sem, pass_send, pass_take, load_sem, store_sem,
 ):
     params, count, rows, length = tangent_ref.shape
     width = length // n
@@ -30,12 +31,28 @@
     me = lax.axis_index("pencil")
     core = lax.axis_index("field")
     first = core * own
+    order = sorted(range(n), key=lambda d: -min(d, n - d))
 
     barrier = pltpu.get_barrier_semaphore()
     for d in range(1, n):
         pl.semaphore_signal(barrier, inc=1, device_id={"pencil": lax.rem(me + d, n)}, device_id_type=MESH)
     for d in range(1, cores):
         pl.semaphore_signal(barrier, inc=1, device_id={"field": lax.rem(core + d, cores)}, device_id_type=MESH)
+
+    def load(k):
+        pairs = ((state_in, state_ref), (d1_in, d1_ref), (d2_in, d2_ref), (filt_in, filt_ref))
+        return pltpu.make_async_copy(*pairs[k], load_sem.at[k])
+
+    def tangent_load(q):
+        return pltpu.make_async_copy(tangent_in.at[q], tangent_ref.at[q], load_sem.at[4 + q])
+
+    def tangent_store(q):
+        return pltpu.make_async_copy(tangent_end.at[q], tangent_out.at[q], store_sem.at[1 + q])
+
+    for k in range(4):
+        load(k).start()
+    for q in range(params):
+        tangent_load(q).start()
 
     def picks(height, offset):
         field = lax.broadcasted_iota(jnp.int32, (height, count), 1)
@@ -119,7 +136,7 @@
             mine = source[pl.ds(first, own), part, :].reshape(own * step, length)
             finish(mine, rate, speed, spreading, target)
 
-        for d in range(n):
+        for d in order:
             state_move(leg, d).start()
 
     def tangent_pass(leg, q, source):
@@ -140,16 +157,19 @@
 
             finish(fields, rate, speed, spreading, target)
 
-        for d in range(n):
+        for d in order:
             tangent_move(leg, q, d).start()
 
     def turned(blocks):
         return blocks.reshape(n * blocks.shape[1], width).T
 
+    for k in range(4):
+        load(k).wait()
     state_pass(0, state_ref)
 
     @pl.loop(0, params)
     def _(q):
+        tangent_load(q).wait()
         tangent_pass(0, q, tangent_ref.at[q])
 
     for d in range(n):
@@ -178,7 +198,7 @@
 
         tangent_pass(1, q, lines)
 
-    for d in range(n):
+    for d in order:
         arrived(state_move(1, d), d)
 
     @pl.loop(0, own)
@@ -195,11 +215,14 @@
 
         @pl.loop(0, count)
         def _(s):
-            tangent_out[q, s] = turned(take_t[1, q, :, s])
+            tangent_end[q, s] = turned(take_t[1, q, :, s])
+
+        tangent_store(q).start()
 
     for d in range(1, cores):
         hand_on(1, state_end.at[pl.ds(first, own)], d).wait_recv()
-    state_out[...] = state_end[...]
+    state_store = pltpu.make_async_copy(state_end, state_out, store_sem.at[0])
+    state_store.start()
 
     for leg in range(2):
         for d in range(1, n):
@@ -214,6 +237,23 @@
             for d in range(1, n):
                 tangent_move(leg, q, d).wait_send()
 
+    state_store.wait()
+
+    @pl.loop(0, params)
+    def _(q):
+        tangent_store(q).wait()
+
+
+def hand_over(state_in, tangent_in, state_out, tangent_out, sems):
+    pairs = [(state_in, state_out)]
+    for q in range(tangent_in.shape[0]):
+        pairs.append((tangent_in.at[q], tangent_out.at[q]))
+    copies = [pltpu.make_async_copy(*pair, sems.at[k]) for k, pair in enumerate(pairs)]
+    for copy in copies:
+        copy.start()
+    for copy in copies:
+        copy.wait()
+
 
 def local(n, cores, state, tangents, d1, d2, filt, advect, diffuse, coef, rates):
     params, count, planes, rows, length = tangents.shape
@@ -222,6 +262,7 @@
     own = count // cores
     bf16, f32 = jnp.bfloat16, jnp.float32
     spot = pl.BlockSpec(memory_space=pltpu.VMEM)
+    far = pl.BlockSpec(memory_space=pl.ANY)
     cells = params * count * rows * length
     call = pl.pallas_call(
         functools.partial(kernel, n, cores, step),
@@ -229,9 +270,15 @@
             jax.ShapeDtypeStruct((count, rows, length), bf16),
             jax.ShapeDtypeStruct((params, count, rows, length), bf16),
         ),
-        in_specs=[spot] * 9,
-        out_specs=(spot, spot),
+        in_specs=[far] * 5 + [spot] * 4,
+        out_specs=(far, far),
         scratch_shapes=[
+            pltpu.VMEM((count, rows, length), bf16),
+            pltpu.VMEM((params, count, rows, length), bf16),
+            pltpu.VMEM((length, length), bf16),
+            pltpu.VMEM((length, length), bf16),
+            pltpu.VMEM((length, length), bf16),
+            pltpu.VMEM((params, count, rows, length), bf16),
             pltpu.VMEM((count * step, count * step), bf16),
             pltpu.VMEM((count * step, count * step), bf16),
             pltpu.VMEM((count * step, count * step), bf16),
@@ -249,6 +296,8 @@
             pltpu.SemaphoreType.DMA((2, params + 1, n)),
             pltpu.SemaphoreType.DMA((2, cores)),
             pltpu.SemaphoreType.DMA((2, cores)),
+            pltpu.SemaphoreType.DMA((4 + params,)),
+            pltpu.SemaphoreType.DMA((1 + params,)),
         ],
         compiler_params=pltpu.CompilerParams(
             collective_id=0, has_side_effects=True, vmem_limit_bytes=56 * 2**20
@@ -257,8 +306,19 @@
             flops=cells * length * 12, bytes_accessed=cells * 4, transcendentals=count * rows * length * 2
         ),
     )
+    copy = pl.pallas_call(
+        hand_over,
+        out_shape=(
+            jax.ShapeDtypeStruct((count, rows, length), bf16),
+            jax.ShapeDtypeStruct((params, count, rows, length), bf16),
+        ),
+        in_specs=[far, far],
+        out_specs=(far, far),
+        scratch_shapes=[pltpu.SemaphoreType.DMA((1 + params,))],
+        compiler_params=pltpu.CompilerParams(vmem_limit_bytes=2**20),
+    )
     outs = [
-        call(state[:, z], tangents[:, :, z], d1, d2, filt, advect, diffuse[None, :], coef, rates)
+        copy(*call(state[:, z], tangents[:, :, z], d1, d2, filt, advect, diffuse[None, :], coef, rates))
         for z in range(planes)
     ]
     return jnp.stack([o[0] for o in outs], 1), jnp.stack([o[1] for o in outs], 2)

time: 224 us -> 220 us (0.982)
  local copies, waits for them, and re-layouts: 6.9 us -> 3.41 us
    unnamed x2 -> x4, local copies, waits for them, and re-layouts: 6.9 us -> 3.41 us
    pallas_call x1, Pallas kernels: 214 us -> 211 us  [local(): call(state[:, z], tangents[:, :, z], d1, d2, filt, advect, diffuse[None,...]
    pallas_call x0 -> x1, Pallas kernels: none -> 2.39 us  [local(): copy(*call(state[:, z], tangents[:, :, z], d1, d2, filt, advect, diffuse[...]
where the time goes in v2:
time: 220 us; the launch traced here: 218 us
  Pallas kernels  214 us (97%)
  local copies, waits for them, and re-layouts  3.41 us (2%)
    pallas_call x1, Pallas kernels, local(): call(state[:, z], tangents[:, :, z], d1, d2, filt, advect, diffuse[None,...  211 us

profile of v2, /device:TPU:0, one launch (start us, length us, event | category | flops | bytes accessed | tf_op | source)
XLA Modules:
  0.0 217.7 jit_solution(6494449877215082859)
XLA Ops:
  0.6 211.2 %shard_map.104 = (bf16[8,128,512]{2,1,0:T(8,128)(2,1)}, bf16[4,8,128,512]{3,2,1,0:T(8,128)(2,1)}) custom-call(bf16[8,128,512]{2,1,0:T(8,128)(2,1)} %bitcast.11, bf16[4,8,128,512]{3,2,1,0:T(8,128)(2,1)} %bitcast.9, bf16[512,512]{1,0:T(8,128)(2,1)} %d1_in.1, bf16[512,512]{1,0:T(8,128)(2,1)} %d2_in.1, bf16[512,512]{1,0:T(8,128)(2,1)} %filt_in.1, ...), custom_call_target="tpu_custom_call" | custom-call | flops 12884901888 | bytes 8388608 | tf_op jit(solution)/shard_map/pallas_call | solution.py:321
  211.9 0.0 copy-start
  211.9 2.2 %copy-done = bf16[4,8,128,512]{3,2,1,0:T(8,128)(2,1)S(1)} copy-done((bf16[4,8,128,512]{3,2,1,0:T(8,128)(2,1)S(1)}, bf16[4,8,128,512]{3,2,1,0:T(8,128)(2,1)}, u32[]{:S(2)}) %copy-start) | copy-done | bytes 4194328
  214.1 0.0 copy-start.1
  214.1 1.2 copy-done.1
  215.3 2.4 %shard_map.105 = (bf16[8,128,512]{2,1,0:T(8,128)(2,1)}, bf16[4,8,128,512]{3,2,1,0:T(8,128)(2,1)}) custom-call(bf16[8,128,512]{2,1,0:T(8,128)(2,1)S(1)} %copy-done.1, bf16[4,8,128,512]{3,2,1,0:T(8,128)(2,1)S(1)} %copy-done), custom_call_target="tpu_custom_call" | custom-call | tf_op jit(solution)/shard_map/pallas_call | solution.py:321
Async XLA Ops:
  211.9 2.2 %copy-start = (bf16[4,8,128,512]{3,2,1,0:T(8,128)(2,1)S(1)}, bf16[4,8,128,512]{3,2,1,0:T(8,128)(2,1)}, u32[]{:S(2)}) copy-start(bf16[4,8,128,512]{3,2,1,0:T(8,128)(2,1)} %get-tuple-element.7.tangent_in) | copy-start | bytes 12582916
  214.1 1.2 copy-start.1

commit v3 on v2

--- a/solution.py
+++ b/solution.py
@@ -116,6 +116,14 @@
         for j in range(n):
             target(j, result[:, j * width : (j + 1) * width])
 
+    def state_sent(leg):
+        for d in range(1, n):
+            state_move(leg, d).wait_send()
+
+    def tangent_sent(leg, q):
+        for d in range(1, n):
+            tangent_move(leg, q, d).wait_send()
+
     def state_pass(leg, source):
         speed = rows_of(advect_ref[leg : leg + 1, :], own_picks)
         spreading = rows_of(diffuse_ref[...], own_picks)
@@ -136,6 +144,8 @@
             mine = source[pl.ds(first, own), part, :].reshape(own * step, length)
             finish(mine, rate, speed, spreading, target)
 
+        if leg == 1:
+            tangent_sent(0, params - 2)
         for d in order:
             state_move(leg, d).start()
 
@@ -157,6 +167,10 @@
 
             finish(fields, rate, speed, spreading, target)
 
+        if leg == 1:
+            pl.when(q == 0)(lambda: tangent_sent(0, params - 1))
+        pl.when(q == 1)(lambda: state_sent(leg))
+        pl.when(q > 1)(lambda: tangent_sent(leg, q - 2))
         for d in order:
             tangent_move(leg, q, d).start()
 
@@ -224,18 +238,11 @@
     state_store = pltpu.make_async_copy(state_end, state_out, store_sem.at[0])
     state_store.start()
 
-    for leg in range(2):
-        for d in range(1, n):
-            state_move(leg, d).wait_send()
-        for d in range(1, cores):
-            hand_on(0, take_s.at[0, core], d).wait_send() if leg == 0 else hand_on(
-                1, state_end.at[pl.ds(first, own)], d
-            ).wait_send()
-
-        @pl.loop(0, params)
-        def _(q):
-            for d in range(1, n):
-                tangent_move(leg, q, d).wait_send()
+    for q in (params - 2, params - 1):
+        tangent_sent(1, q)
+    for d in range(1, cores):
+        hand_on(0, take_s.at[0, core], d).wait_send()
+        hand_on(1, state_end.at[pl.ds(first, own)], d).wait_send()
 
     state_store.wait()
 
@@ -312,7 +319,7 @@
             jax.ShapeDtypeStruct((count, rows, length), bf16),
             jax.ShapeDtypeStruct((params, count, rows, length), bf16),
         ),
-        in_specs=[far, far],
+        in_specs=[pl.BlockSpec(memory_space=pltpu.HBM)] * 2,
         out_specs=(far, far),
         scratch_shapes=[pltpu.SemaphoreType.DMA((1 + params,))],
         compiler_params=pltpu.CompilerParams(vmem_limit_bytes=2**20),

time: 220 us -> 220 us (level)
  no operation moved by 1% of the time
where the time goes in v3:
time: 220 us; the launch traced here: 218 us
  Pallas kernels  214 us (97%)
  local copies, waits for them, and re-layouts  3.41 us (2%)
    pallas_call x1, Pallas kernels, local(): call(state[:, z], tangents[:, :, z], d1, d2, filt, advect, diffuse[None,...  211 us

profile of v3, /device:TPU:0, one launch (start us, length us, event | category | flops | bytes accessed | tf_op | source)
XLA Modules:
  0.0 217.6 jit_solution(18034469519173635704)
XLA Ops:
  0.6 211.1 %shard_map.104 = (bf16[8,128,512]{2,1,0:T(8,128)(2,1)}, bf16[4,8,128,512]{3,2,1,0:T(8,128)(2,1)}) custom-call(bf16[8,128,512]{2,1,0:T(8,128)(2,1)} %bitcast.11, bf16[4,8,128,512]{3,2,1,0:T(8,128)(2,1)} %bitcast.9, bf16[512,512]{1,0:T(8,128)(2,1)} %d1_in.1, bf16[512,512]{1,0:T(8,128)(2,1)} %d2_in.1, bf16[512,512]{1,0:T(8,128)(2,1)} %filt_in.1, ...), custom_call_target="tpu_custom_call" | custom-call | flops 12884901888 | bytes 8388608 | tf_op jit(solution)/shard_map/pallas_call | solution.py:328
  211.8 0.0 copy-start
  211.8 2.2 %copy-done = bf16[4,8,128,512]{3,2,1,0:T(8,128)(2,1)S(1)} copy-done((bf16[4,8,128,512]{3,2,1,0:T(8,128)(2,1)S(1)}, bf16[4,8,128,512]{3,2,1,0:T(8,128)(2,1)}, u32[]{:S(2)}) %copy-start) | copy-done | bytes 4194328
  214.0 0.0 copy-start.1
  214.0 1.2 copy-done.1
  215.2 2.4 %shard_map.105 = (bf16[8,128,512]{2,1,0:T(8,128)(2,1)}, bf16[4,8,128,512]{3,2,1,0:T(8,128)(2,1)}) custom-call(bf16[8,128,512]{2,1,0:T(8,128)(2,1)S(1)} %copy-done.1, bf16[4,8,128,512]{3,2,1,0:T(8,128)(2,1)S(1)} %copy-done), custom_call_target="tpu_custom_call" | custom-call | tf_op jit(solution)/shard_map/pallas_call | solution.py:328
Async XLA Ops:
  211.8 2.2 %copy-start = (bf16[4,8,128,512]{3,2,1,0:T(8,128)(2,1)S(1)}, bf16[4,8,128,512]{3,2,1,0:T(8,128)(2,1)}, u32[]{:S(2)}) copy-start(bf16[4,8,128,512]{3,2,1,0:T(8,128)(2,1)} %get-tuple-element.7.tangent_in) | copy-start | bytes 12582916
  214.0 1.2 copy-start.1

commit v4 on v3

--- a/solution.py
+++ b/solution.py
@@ -23,7 +23,7 @@
     state_ref, tangent_ref, d1_ref, d2_ref, filt_ref, tangent_end,
     rates_hi, rates_lo, coef_mix, coef_own, act, slopes, lines, state_lines, state_end,
     send_s, send_t, take_s, take_t,
-    send_sem, take_sem, pass_send, pass_take, load_sem, store_sem,
+    send_sem, take_sem, pass_send, pass_take, load_sem, store_sem, part_send, part_take,
 ):
     params, count, rows, length = tangent_ref.shape
     width = length // n
@@ -90,6 +90,19 @@
             device_id={"pencil": dest}, device_id_type=MESH,
         )
 
+    def part_move(c, d):
+        part = pl.ds(c * step, step)
+        dest = lax.rem(me + d, n)
+        if d == 0:
+            return pltpu.make_async_copy(
+                send_s.at[0, me, :, part], take_s.at[0, core, me, :, part], part_take.at[c, 0]
+            )
+        return pltpu.make_async_remote_copy(
+            src_ref=send_s.at[0, dest, :, part], dst_ref=take_s.at[0, core, me, :, part],
+            send_sem=part_send.at[c, d], recv_sem=part_take.at[c, d],
+            device_id={"pencil": dest}, device_id_type=MESH,
+        )
+
     def state_move(leg, d):
         return move(leg, 0, send_s.at[leg], take_s.at[leg, core], d)
 
@@ -118,7 +131,11 @@
 
     def state_sent(leg):
         for d in range(1, n):
-            state_move(leg, d).wait_send()
+            if leg == 1:
+                state_move(leg, d).wait_send()
+            else:
+                for c in range(rows // step):
+                    part_move(c, d).wait_send()
 
     def tangent_sent(leg, q):
         for d in range(1, n):
@@ -144,10 +161,14 @@
             mine = source[pl.ds(first, own), part, :].reshape(own * step, length)
             finish(mine, rate, speed, spreading, target)
 
+            if leg == 0:
+                for d in order:
+                    part_move(c, d).start()
+
         if leg == 1:
             tangent_sent(0, params - 2)
-        for d in order:
-            state_move(leg, d).start()
+            for d in order:
+                state_move(leg, d).start()
 
     def tangent_pass(leg, q, source):
         speed = rows_of(advect_ref[leg : leg + 1, :], all_picks)
@@ -187,7 +208,8 @@
         tangent_pass(0, q, tangent_ref.at[q])
 
     for d in range(n):
-        arrived(state_move(0, d), d)
+        for c in range(rows // step):
+            arrived(part_move(c, d), d)
     for d in range(1, cores):
         hand_on(0, take_s.at[0, core], d).start()
     for d in range(1, cores):
@@ -305,6 +327,8 @@
             pltpu.SemaphoreType.DMA((2, cores)),
             pltpu.SemaphoreType.DMA((4 + params,)),
             pltpu.SemaphoreType.DMA((1 + params,)),
+            pltpu.SemaphoreType.DMA((rows // step, n)),
+            pltpu.SemaphoreType.DMA((rows // step, n)),
         ],
         compiler_params=pltpu.CompilerParams(
             collective_id=0, has_side_effects=True, vmem_limit_bytes=56 * 2**20
@@ -322,7 +346,7 @@
         in_specs=[pl.BlockSpec(memory_space=pltpu.HBM)] * 2,
         out_specs=(far, far),
         scratch_shapes=[pltpu.SemaphoreType.DMA((1 + params,))],
-        compiler_params=pltpu.CompilerParams(vmem_limit_bytes=2**20),
+        compiler_params=pltpu.CompilerParams(vmem_limit_bytes=60 * 2**20),
     )
     outs = [
         copy(*call(state[:, z], tangents[:, :, z], d1, d2, filt, advect, diffuse[None, :], coef, rates))

time: 220 us -> 372 us (1.69)
  Pallas kernels: 214 us -> 369 us
    pallas_call x1, Pallas kernels: 2.39 us -> 160 us  [local(): copy(*call(state[:, z], tangents[:, :, z], d1, d2, filt, advect, diffuse[...]
where the time goes in v4:
time: 372 us; the launch traced here: 370 us
  Pallas kernels  369 us (99%)
    pallas_call x1, Pallas kernels, local(): call(state[:, z], tangents[:, :, z], d1, d2, filt, advect, diffuse[None,...  209 us
    pallas_call x1, Pallas kernels, local(): copy(*call(state[:, z], tangents[:, :, z], d1, d2, filt, advect, diffuse[...  160 us

profile of v4, /device:TPU:0, one launch (start us, length us, event | category | flops | bytes accessed | tf_op | source)
XLA Modules:
  0.0 369.6 jit_solution(16808396448189964072)
XLA Ops:
  0.6 209.0 %shard_map.104 = (bf16[8,128,512]{2,1,0:T(8,128)(2,1)}, bf16[4,8,128,512]{3,2,1,0:T(8,128)(2,1)}) custom-call(bf16[8,128,512]{2,1,0:T(8,128)(2,1)} %bitcast.11, bf16[4,8,128,512]{3,2,1,0:T(8,128)(2,1)} %bitcast.9, bf16[512,512]{1,0:T(8,128)(2,1)} %d1_in.1, bf16[512,512]{1,0:T(8,128)(2,1)} %d2_in.1, bf16[512,512]{1,0:T(8,128)(2,1)} %filt_in.1, ...), custom_call_target="tpu_custom_call" | custom-call | flops 12884901888 | bytes 8388608 | tf_op jit(solution)/shard_map/pallas_call | solution.py:352
  209.7 160.0 %shard_map.105 = (bf16[8,128,512]{2,1,0:T(8,128)(2,1)}, bf16[4,8,128,512]{3,2,1,0:T(8,128)(2,1)}) custom-call(bf16[8,128,512]{2,1,0:T(8,128)(2,1)} %get-tuple-element.6.state_in, bf16[4,8,128,512]{3,2,1,0:T(8,128)(2,1)} %get-tuple-element.7.tangent_in), custom_call_target="tpu_custom_call" | custom-call | tf_op jit(solution)/shard_map/pallas_call | solution.py:352
